TPU v7x, 512 devices: a whole 4x8x8 slice. The times are simulated.
512 devices in a mesh: vocab: 16 (over y, core), docs: 32 (over x, z).
Axes of the slice: x: 4, y: 8, z: 8, core: 2. Of those that a mesh axis runs over, the one named last changes fastest.
Arguments:
- counts: bfloat16 [65536, 4, 128], P(('vocab', 'docs')), may hold values from 0 to 2
- doc_owner: int32 [65536, 4], P(('vocab', 'docs')), may hold values from 0 to 511, all different within a row; in each aligned block of 128 rows (0 to 127, 128 to 255, ...) at most 2 rows name the same one
- doc_sub: int32 [65536, 4], P(('vocab', 'docs')), may hold values from 0 to 7
- doc_len: int32 [65536], P(('vocab', 'docs')), may hold values from 256 to 1023
- first_weight: bfloat16 [524288, 2048], P(('vocab', 'docs')), may hold values from -0.25 to 0.25
- first_bias: float32 [2048], replicated, may hold values from -3 to 3
- head_weight: bfloat16 [2048, 1536], P('vocab', 'docs'), may hold values from -0.125 to 0.125
- head_bias: float32 [1536], replicated, may hold values from -4 to 4
- factor: bfloat16 [1536, 1536], P('vocab', 'docs'), as said below
- noise_draw: bfloat16 [65536, 1536], P(('vocab', 'docs')), may hold values from -5 to 5
Outputs:
- sample: bfloat16 [65536, 1536], P(('vocab', 'docs'))
Inputs may be any that keep to these rules, and one draw needn't show every extreme that they name: `doc_owner`: each document names 4 different owners. The documents of one device name one owner in at most 2 slots, and on some device some owner is named in exactly 2 slots. `factor`: lower triangular; diagonal entries lie between 0.5 and 1.5.
All inputs are finite; a program needn't handle non-finite values.
Results may differ from a plain program's by a relative error of at most 0.0038.
Values may be sent and summed in bfloat16 or wider, within the bound.
No kernel may reach another device: no remote copies, remote signals or barrier semaphores. Data moves between devices by JAX's collectives and lax.ppermute only.
A program may use at most 128 MiB of HBM per device.

v0:
```python
import jax
import jax.numpy as jnp
from jax import lax
from jax.sharding import PartitionSpec as P


def local(
    counts,
    doc_owner,
    doc_sub,
    doc_len,
    first_weight,
    first_bias,
    head_weight,
    head_bias,
    factor,
    noise_draw,
):
    vocab_devices = lax.axis_size("vocab")
    docs_devices = lax.axis_size("docs")
    device_count = vocab_devices * docs_devices
    docs_here, slot_count, block_width = counts.shape
    hidden_width = first_weight.shape[1]
    per_owner = first_weight.shape[0] // block_width
    capacity = max(2, 2 * docs_here * slot_count // device_count)
    owner_flat = doc_owner.reshape(-1)
    onehot = (owner_flat[:, None] == jnp.arange(device_count, dtype=jnp.int32)[None, :]).astype(
        jnp.int32
    )
    position = jnp.sum(jnp.cumsum(onehot, axis=0) * onehot, axis=1) - 1
    slot_index = owner_flat * capacity + position
    flat_rows = counts.reshape(-1, block_width)
    send_rows = (
        jnp.zeros((device_count * capacity, block_width), counts.dtype)
        .at[slot_index]
        .set(flat_rows)
    )
    send_sub = (
        jnp.zeros((device_count * capacity,), jnp.bfloat16)
        .at[slot_index]
        .set(doc_sub.reshape(-1).astype(jnp.bfloat16))
    )
    send_rows = send_rows.reshape(vocab_devices, docs_devices, capacity, block_width)
    send_sub = send_sub.reshape(vocab_devices, docs_devices, capacity)
    got_rows, got_sub = (
        lax.all_to_all(
            lax.all_to_all(send_rows, "vocab", split_axis=0, concat_axis=0, tiled=True),
            "docs",
            split_axis=1,
            concat_axis=1,
            tiled=True,
        ),
        lax.all_to_all(
            lax.all_to_all(send_sub, "vocab", split_axis=0, concat_axis=0, tiled=True),
            "docs",
            split_axis=1,
            concat_axis=1,
            tiled=True,
        ),
    )
    got_rows = got_rows.reshape(-1, block_width)
    got_sub = got_sub.reshape(-1).astype(jnp.int32)
    select = (got_sub[:, None] == jnp.arange(per_owner, dtype=jnp.int32)[None, :]).astype(
        jnp.bfloat16
    )
    spread = (select[:, :, None] * got_rows[:, None, :]).reshape(-1, per_owner * block_width)
    owner_terms = jnp.dot(spread, first_weight, preferred_element_type=jnp.float32).astype(
        jnp.bfloat16
    )
    owner_terms = owner_terms.reshape(vocab_devices, docs_devices, capacity, hidden_width)
    returned = lax.all_to_all(
        lax.all_to_all(owner_terms, "vocab", split_axis=0, concat_axis=0, tiled=True),
        "docs",
        split_axis=1,
        concat_axis=1,
        tiled=True,
    )
    returned = returned.reshape(-1, hidden_width)
    own_rows = returned[slot_index].reshape(docs_here, slot_count, hidden_width).astype(jnp.float32)
    summed = jnp.sum(own_rows, axis=1)
    length_scale = 128.0 * slot_count / doc_len.astype(jnp.float32)
    hidden = jax.nn.softplus(summed * length_scale[:, None] + first_bias).astype(jnp.bfloat16)
    panel_rows = lax.all_gather(head_weight, "docs", axis=1, tiled=True)
    location = jnp.dot(
        hidden,
        lax.all_gather(panel_rows, "vocab", axis=0, tiled=True),
        preferred_element_type=jnp.float32,
    )
    factor_panel = lax.all_gather(factor, "docs", axis=1, tiled=True)
    correlated = lax.dot_general(
        noise_draw,
        lax.all_gather(factor_panel, "vocab", axis=0, tiled=True),
        (((1,), (1,)), ((), ())),
        preferred_element_type=jnp.float32,
    )
    return (location + head_bias + correlated).astype(jnp.bfloat16)


def solution(mesh):
    return jax.shard_map(
        local,
        mesh=mesh,
        in_specs=(
            P(("vocab", "docs"), None, None),
            P(("vocab", "docs"), None),
            P(("vocab", "docs"), None),
            P(("vocab", "docs")),
            P(("vocab", "docs"), None),
            P(),
            P("vocab", "docs"),
            P(),
            P("vocab", "docs"),
            P(("vocab", "docs"), None),
        ),
        out_specs=P(("vocab", "docs"), None),
        check_vma=False,
    )
```

profile of v0, /device:TPU:1, one launch (start us, length us, event | category | flops | bytes accessed | tf_op | source)
XLA Modules:
  0.0 425.2 jit_solution(10619048773508162734)
XLA Ops:
  6.5 50.0 %all_gather.12 = bf16[128,1536]{0,1:T(8,128)(2,1)} all-gather(bf16[128,48]{0,1:T(8,128)(2,1)} %param.16), channel_id=1, replica_groups=mesh['vocab'=16,'docs'=32] {'docs'}, dimensions={1}, use_global_device_ids=true | all-gather | bytes 405504 | tf_op jit(solution)/shard_map/all_gather | solution.py:83
  56.6 0.8 copy.58
  57.4 0.1 eq.46
  57.5 0.1 eq.42
  57.6 0.1 copy.60
  57.7 0.3 fusion.5
  58.1 0.1 broadcast_add_fusion
  58.2 0.3 copy.61
  58.5 0.1 copy.57
  58.6 0.1 mul.48
  58.8 0.1 copy.62
  58.9 0.1 reshape.128
  59.0 0.3 fusion.4
  59.3 3.8 scatter_custom_fusion
  63.1 0.3 reshape.109
  63.3 0.8 copy.63
  64.1 18.7 %all-to-all-start = ((bf16[16,32,2]{1,2,0:T(2,128)(2,1)}), bf16[16,32,2]{1,2,0:T(2,128)(2,1)S(1)}, u32[]{:S(2)}, u32[]{:S(2)}) async-start(bf16[16,32,2]{1,2,0:T(2,128)(2,1)} %copy.63), calls=%async_computation | async-start | bytes 16384 | tf_op jit(solution)/shard_map/all_to_all | solution.py:54
  82.9 2.8 scatter_custom_fusion.1
  85.6 4.3 %all-to-all-done = bf16[16,32,2]{1,2,0:T(2,128)(2,1)S(1)} async-done(((bf16[16,32,2]{1,2,0:T(2,128)(2,1)}), bf16[16,32,2]{1,2,0:T(2,128)(2,1)S(1)}, u32[]{:S(2)}, u32[]{:S(2)}) %all-to-all-start) | async-done | bytes 2080 | tf_op jit(solution)/shard_map/all_to_all | solution.py:54
  90.0 3.9 all-to-all-start.2
  93.9 0.7 copy.64
  94.5 13.3 %all-to-all-done.2 = bf16[16,32,2,128]{3,2,1,0:T(2,128)(2,1)S(1)} async-done(((bf16[16,32,2,128]{3,2,1,0:T(2,128)(2,1)}), bf16[16,32,2,128]{3,2,1,0:T(2,128)(2,1)S(1)}, u32[]{:S(2)}, u32[]{:S(2)}) %all-to-all-start.2) | async-done | bytes 262176 | tf_op jit(solution)/shard_map/all_to_all | solution.py:47
  107.9 4.7 %all-to-all-start.1 = ((bf16[16,32,2]{0,2,1:T(2,128)(2,1)}), bf16[16,32,2]{0,2,1:T(2,128)(2,1)S(1)}, u32[]{:S(2)}, u32[]{:S(2)}) async-start(bf16[16,32,2]{0,2,1:T(2,128)(2,1)} %copy.64), calls=%async_computation.1 | async-start | bytes 32768 | tf_op jit(solution)/shard_map/all_to_all | solution.py:53
  112.6 0.9 copy.67
  113.5 7.7 %all-to-all-done.1 = bf16[16,32,2]{0,2,1:T(2,128)(2,1)S(1)} async-done(((bf16[16,32,2]{0,2,1:T(2,128)(2,1)}), bf16[16,32,2]{0,2,1:T(2,128)(2,1)S(1)}, u32[]{:S(2)}, u32[]{:S(2)}) %all-to-all-start.1) | async-done | bytes 2080 | tf_op jit(solution)/shard_map/all_to_all | solution.py:53
  121.2 4.0 all-to-all-start.3
  125.4 0.2 copy.66
  125.6 0.2 reshape.114
  125.7 0.2 fusion.12
  126.0 8.8 %all-to-all-done.3 = bf16[16,32,2,128]{3,2,0,1:T(2,128)(2,1)S(1)} async-done(((bf16[16,32,2,128]{3,2,0,1:T(2,128)(2,1)}), bf16[16,32,2,128]{3,2,0,1:T(2,128)(2,1)S(1)}, u32[]{:S(2)}, u32[]{:S(2)}) %all-to-all-start.3) | async-done | bytes 262176 | tf_op jit(solution)/shard_map/all_to_all | solution.py:46
  134.8 0.2 copy.68
  135.0 3.5 broadcast_multiply_fusion
  138.5 8.3 %convolution_convert_fusion = bf16[1024,2048]{1,0:T(8,128)(2,1)} fusion(bf16[1024,2048]{1,0:T(8,128)(2,1)} %param.14, bf16[128,8,8,128]{3,2,1,0:T(8,128)(2,1)S(1)} %bitcast.26), kind=kOutput, calls=%fused_computation.3 | convolution fusion | flops 4297064448 | bytes 10485760 | tf_op jit(solution)/shard_map/dot_general | solution.py:67
  146.8 7.6 %reshape.112 = bf16[16,32,2,2048]{3,2,1,0:T(2,128)(2,1)} reshape(bf16[1024,2048]{1,0:T(8,128)(2,1)} %convolution_convert_fusion) | data formatting | bytes 8388608 | tf_op jit(solution)/shard_map/reshape | solution.py:70
  154.4 8.1 %all-to-all-start.4 = ((bf16[16,32,2,2048]{3,2,1,0:T(2,128)(2,1)}), bf16[16,32,2,2048]{3,2,1,0:T(2,128)(2,1)}, u32[]{:S(2)}, u32[]{:S(2)}) async-start(bf16[16,32,2,2048]{3,2,1,0:T(2,128)(2,1)} %reshape.112), calls=%async_computation.4 | async-start | bytes 8388608 | tf_op jit(solution)/shard_map/all_to_all | solution.py:72
  162.5 40.7 %all_gather.14 = bf16[96,1536]{0,1:T(8,128)(2,1)S(1)} all-gather(bf16[96,48]{0,1:T(8,128)(2,1)S(1)} %copy-done.1), channel_id=1, replica_groups=mesh['vocab'=16,'docs'=32] {'docs'}, dimensions={1}, use_global_device_ids=true | all-gather | bytes 304128 | tf_op jit(solution)/shard_map/all_gather | solution.py:89
  203.3 0.9 copy.71
  204.2 65.5 %all-to-all-done.4 = bf16[16,32,2,2048]{3,2,1,0:T(2,128)(2,1)} async-done(((bf16[16,32,2,2048]{3,2,1,0:T(2,128)(2,1)}), bf16[16,32,2,2048]{3,2,1,0:T(2,128)(2,1)}, u32[]{:S(2)}, u32[]{:S(2)}) %all-to-all-start.4) | async-done | bytes 4194336 | tf_op jit(solution)/shard_map/all_to_all | solution.py:72
  269.7 8.8 %copy.69 = bf16[16,32,2,2048]{3,2,0,1:T(2,128)(2,1)} copy(bf16[16,32,2,2048]{3,2,1,0:T(2,128)(2,1)} %all-to-all-done.4) | data formatting | bytes 8388608 | tf_op jit(solution)/shard_map/all_to_all | solution.py:72
  278.5 5.2 %all-to-all-start.5 = ((bf16[16,32,2,2048]{3,2,0,1:T(2,128)(2,1)}), bf16[16,32,2,2048]{3,2,0,1:T(2,128)(2,1)}, u32[]{:S(2)}, u32[]{:S(2)}) async-start(bf16[16,32,2,2048]{3,2,0,1:T(2,128)(2,1)} %copy.69), calls=%async_computation.5 | async-start | bytes 8388608 | tf_op jit(solution)/shard_map/all_to_all | solution.py:71
  283.8 94.4 %all-to-all-done.5 = bf16[16,32,2,2048]{3,2,0,1:T(2,128)(2,1)} async-done(((bf16[16,32,2,2048]{3,2,0,1:T(2,128)(2,1)}), bf16[16,32,2,2048]{3,2,0,1:T(2,128)(2,1)}, u32[]{:S(2)}, u32[]{:S(2)}) %all-to-all-start.5) | async-done | bytes 4194336 | tf_op jit(solution)/shard_map/all_to_all | solution.py:71
  378.2 8.0 %copy.70 = bf16[16,32,2,2048]{3,2,1,0:T(2,128)(2,1)} copy(bf16[16,32,2,2048]{3,2,0,1:T(2,128)(2,1)} %all-to-all-done.5) | data formatting | bytes 8388608 | tf_op jit(solution)/shard_map/all_to_all | solution.py:71
  386.2 7.2 %reshape.113 = bf16[1024,2048]{1,0:T(8,128)(2,1)} reshape(bf16[16,32,2,2048]{3,2,1,0:T(2,128)(2,1)} %copy.70) | data formatting | bytes 8388608 | tf_op jit(solution)/shard_map/reshape | solution.py:78
  393.4 7.1 %gather_fusion = bf16[512,2048]{1,0:T(8,128)(2,1)S(1)} fusion(bf16[1024,2048]{1,0:T(8,128)(2,1)} %reshape.113, s32[1024]{0:T(1024)S(1)} %pad_clamp_fusion), kind=kCustom, calls=%fused_computation | custom fusion | bytes 4196352 | tf_op jit(solution)/shard_map/gather | solution.py:79
  400.6 3.0 reshape.115
  403.6 4.8 %reduce_sum.19 = f32[128,2048]{1,0:T(8,128)S(1)} reduce(f32[128,4,2048]{2,1,0:T(4,128)} %reshape.115, f32[]{:T(128)} %constant.6.clone.1), dimensions={1}, to_apply=%region_5.6 | reduce | flops 786432 | bytes 5242884 | tf_op jit(solution)/shard_map/reduce_sum | solution.py:80
  408.5 5.1 %convolution_add_fusion.1 = f32[128,1536]{1,0:T(8,128)S(1)} fusion(bf16[2048,1536]{0,1:T(8,128)(2,1)} %all-gather.3.cloned.1.call-done, f32[128,2048]{1,0:T(8,128)S(1)} %reduce_sum.19, f32[2048]{0:T(1024)S(1)} %copy-done.4, f32[128]{0:T(128)S(1)} %convert_divide_fusion, f32[1536]{0:T(1024)S(1)} %copy-done.5), kind=kOutput, calls=%fused_computation.6 | convolution fusion | flops 807862272 | bytes 8141312 | tf_op jit(solution)/shard_map/dot_general | solution.py:84
  413.7 4.7 %fusion = bf16[128,1536]{1,0:T(8,128)(2,1)} fusion(f32[128,1536]{1,0:T(8,128)S(1)} %convolution_add_fusion.1, bf16[128,1536]{1,0:T(8,128)(2,1)S(1)} %copy-done, bf16[1536,1536]{1,0:T(8,128)(2,1)} %all-gather.5.cloned.1.call-done), kind=kOutput, calls=%fused_computation.7 | convolution fusion | flops 604372992 | bytes 6291456 | tf_op jit(solution)/shard_map/dot_general | solution.py:90
  (32 shorter events, 0.3 us)
Async XLA Ops:
  6.5 407.1 %copy-start = (bf16[128,1536]{1,0:T(8,128)(2,1)S(1)}, bf16[128,1536]{1,0:T(8,128)(2,1)}, u32[]{:S(2)}) copy-start(bf16[128,1536]{1,0:T(8,128)(2,1)} %param.19) | copy-start | bytes 1179652
  6.5 52.0 %copy-start.2 = (s32[128,4]{0,1:T(4,128)S(1)}, s32[128,4]{0,1:T(4,128)}, u32[]{:S(2)}) copy-start(s32[128,4]{0,1:T(4,128)} %param.11) | copy-start | bytes 6148
  6.5 52.2 %copy-start.3 = (s32[128,4]{0,1:T(4,128)S(1)}, s32[128,4]{0,1:T(4,128)}, u32[]{:S(2)}) copy-start(s32[128,4]{0,1:T(4,128)} %param.12) | copy-start | bytes 6148
  6.5 402.0 %all-gather.3.cloned.1.call-start = ((), (), s32[]{:S(2)}) async-start(), calls=%async_computation.6 | async-start | bytes 6684672 | tf_op jit(solution)/shard_map/all_gather | solution.py:86
  64.1 25.8 %all-to-all-start = ((bf16[16,32,2]{1,2,0:T(2,128)(2,1)}), bf16[16,32,2]{1,2,0:T(2,128)(2,1)S(1)}, u32[]{:S(2)}, u32[]{:S(2)}) async-start(bf16[16,32,2]{1,2,0:T(2,128)(2,1)} %copy.63), calls=%async_computation | async-start | bytes 16384 | tf_op jit(solution)/shard_map/all_to_all | solution.py:54
  90.0 17.9 %all-to-all-start.2 = ((bf16[16,32,2,128]{3,2,1,0:T(2,128)(2,1)}), bf16[16,32,2,128]{3,2,1,0:T(2,128)(2,1)S(1)}, u32[]{:S(2)}, u32[]{:S(2)}) async-start(bf16[16,32,2,128]{3,2,1,0:T(2,128)(2,1)} %bitcast.6), calls=%async_computation.2 | async-start | bytes 524288 | tf_op jit(solution)/shard_map/all_to_all | solution.py:47
  107.9 13.3 %all-to-all-start.1 = ((bf16[16,32,2]{0,2,1:T(2,128)(2,1)}), bf16[16,32,2]{0,2,1:T(2,128)(2,1)S(1)}, u32[]{:S(2)}, u32[]{:S(2)}) async-start(bf16[16,32,2]{0,2,1:T(2,128)(2,1)} %copy.64), calls=%async_computation.1 | async-start | bytes 32768 | tf_op jit(solution)/shard_map/all_to_all | solution.py:53
  121.2 13.5 %all-to-all-start.3 = ((bf16[16,32,2,128]{3,2,0,1:T(2,128)(2,1)}), bf16[16,32,2,128]{3,2,0,1:T(2,128)(2,1)S(1)}, u32[]{:S(2)}, u32[]{:S(2)}) async-start(bf16[16,32,2,128]{3,2,0,1:T(2,128)(2,1)} %copy.67), calls=%async_computation.3 | async-start | bytes 524288 | tf_op jit(solution)/shard_map/all_to_all | solution.py:46
  154.4 8.1 %copy-start.1 = (bf16[96,48]{0,1:T(8,128)(2,1)S(1)}, bf16[96,48]{0,1:T(8,128)(2,1)}, u32[]{:S(2)}) copy-start(bf16[96,48]{0,1:T(8,128)(2,1)} %param.18) | copy-start | bytes 27652
  154.4 115.3 %all-to-all-start.4 = ((bf16[16,32,2,2048]{3,2,1,0:T(2,128)(2,1)}), bf16[16,32,2,2048]{3,2,1,0:T(2,128)(2,1)}, u32[]{:S(2)}, u32[]{:S(2)}) async-start(bf16[16,32,2,2048]{3,2,1,0:T(2,128)(2,1)} %reshape.112), calls=%async_computation.4 | async-start | bytes 8388608 | tf_op jit(solution)/shard_map/all_to_all | solution.py:72
  162.5 251.2 %all-gather.5.cloned.1.call-start = ((), (), s32[]{:S(2)}) async-start(), calls=%async_computation.7 | async-start | bytes 5013504 | tf_op jit(solution)/shard_map/all_gather | solution.py:92
  278.5 5.2 %copy-start.6 = (s32[128]{0:T(128)S(1)}, s32[128]{0:T(128)}, u32[]{:S(2)}) copy-start(s32[128]{0:T(128)} %param.13) | copy-start | bytes 1540
  278.5 99.7 %all-to-all-start.5 = ((bf16[16,32,2,2048]{3,2,0,1:T(2,128)(2,1)}), bf16[16,32,2,2048]{3,2,0,1:T(2,128)(2,1)}, u32[]{:S(2)}, u32[]{:S(2)}) async-start(bf16[16,32,2,2048]{3,2,0,1:T(2,128)(2,1)} %copy.69), calls=%async_computation.5 | async-start | bytes 8388608 | tf_op jit(solution)/shard_map/all_to_all | solution.py:71
  403.6 4.9 %copy-start.4 = (f32[2048]{0:T(1024)S(1)}, f32[2048]{0:T(1024)}, u32[]{:S(2)}) copy-start(f32[2048]{0:T(1024)} %param.15) | copy-start | bytes 24580
  403.6 4.9 %copy-start.5 = (f32[1536]{0:T(1024)S(1)}, f32[1536]{0:T(1024)}, u32[]{:S(2)}) copy-start(f32[1536]{0:T(1024)} %param.17) | copy-start | bytes 18436
Sparse Core Ops, SparseCore 0:
  56.7 72.7 all-gather.2
  204.3 78.6 all-gather.4
where the time goes:
time: 426 us; the launch traced here: 425 us
  waiting for transfers between devices  194 us (46%)
  blocking collectives  90.8 us (21%)
  local copies, waits for them, and re-layouts  54.5 us (13%)
  starting transfers between devices  44.7 us (10%)
  matrix products  18.1 us (4%)
  between operations  13.7 us (3%)
  other arithmetic  9.24 us (2%)
    all_to_all x1, waiting for transfers between devices, local(): lax.all_to_all(lax.all_to_all(owner_terms, 'vocab', split_axis=0, concat_...  94.4 us
    all_to_all x1, waiting for transfers between devices, local(): lax.all_to_all(owner_terms, 'vocab', split_axis=0, concat_axis=0, tiled=T...  65.5 us
    all_gather x1, blocking collectives, local(): panel_rows = lax.all_gather(head_weight, 'docs', axis=1, tiled=True)  50 us
    all_gather x1, blocking collectives, local(): factor_panel = lax.all_gather(factor, 'docs', axis=1, tiled=True)  40.7 us
    all_to_all x1, starting transfers between devices, local(): lax.all_to_all(send_sub, 'vocab', split_axis=0, concat_axis=0, tiled=True)  18.7 us
    all_to_all x1, waiting for transfers between devices, local(): lax.all_to_all(send_rows, 'vocab', split_axis=0, concat_axis=0, tiled=True)  13.3 us
    all_to_all x1, waiting for transfers between devices, local(): lax.all_to_all(lax.all_to_all(send_rows, 'vocab', split_axis=0, concat_ax...  8.81 us
    all_to_all x1, local copies, waits for them, and re-layouts, local(): lax.all_to_all(owner_terms, 'vocab', split_axis=0, concat_axis=0, tiled=T...  8.8 us
  transfers between devices with their start and end apart: 8, of which 6 were waited for; matrix products, arithmetic and copies ran while one was open for 18% of the time, Pallas kernels for 0%

commit v1 on v0

--- a/solution.py
+++ b/solution.py
@@ -2,6 +2,7 @@
 import jax.numpy as jnp
 from jax import lax
 from jax.sharding import PartitionSpec as P
+from jax.lax import all_to_all, axis_size
 
 
 def local(
@@ -86,7 +87,15 @@
         lax.all_gather(panel_rows, "vocab", axis=0, tiled=True),
         preferred_element_type=jnp.float32,
     )
-    factor_panel = lax.all_gather(factor, "docs", axis=1, tiled=True)
+    factor_panel = jnp.concatenate(
+        all_to_all(
+            jnp.stack(axis_size("docs") * [factor], 0),
+            axis_name="docs",
+            split_axis=0,
+            concat_axis=0,
+        ),
+        1,
+    )
     correlated = lax.dot_general(
         noise_draw,
         lax.all_gather(factor_panel, "vocab", axis=0, tiled=True),

time: 426 us -> 446 us (1.047)
  waiting for transfers between devices: 194 us -> 242 us
  blocking collectives: 90.8 us -> 49.2 us
  starting transfers between devices: 44.7 us -> 54.7 us
    all_to_all x1, waiting for transfers between devices: 65.5 us -> 115 us  [local(): lax.all_to_all(owner_terms, 'vocab', split_axis=0, concat_axis=0, tiled=T...]
    all_gather x1 -> x0, blocking collectives: 40.7 us -> none  [local(): factor_panel = lax.all_gather(factor, 'docs', axis=1, tiled=True)]
    all_to_all x0 -> x1, starting transfers between devices: none -> 6.26 us  [local(): all_to_all(jnp.stack(axis_size('docs') * [factor], 0), axis_name='docs',...]
    all_to_all x1, starting transfers between devices: 5.22 us -> 9.81 us  [local(): lax.all_to_all(lax.all_to_all(owner_terms, 'vocab', split_axis=0, concat_...]
  transfers between devices with their start and end apart: 8 -> 9, of which waited for: 6 -> 6; matrix products, arithmetic and copies ran while one was open for 18% -> 18% of each run, Pallas kernels for 0% -> 0%
where the time goes in v1:
time: 446 us; the launch traced here: 442 us
  waiting for transfers between devices  242 us (54%)
  local copies, waits for them, and re-layouts  55.2 us (12%)
  starting transfers between devices  54.7 us (12%)
  blocking collectives  49.2 us (11%)
  matrix products  18.1 us (4%)
  between operations  13.7 us (3%)
  other arithmetic  9.24 us (2%)
    all_to_all x1, waiting for transfers between devices, local(): lax.all_to_all(owner_terms, 'vocab', split_axis=0, concat_axis=0, tiled=T...  115 us
    all_to_all x1, waiting for transfers between devices, local(): lax.all_to_all(lax.all_to_all(owner_terms, 'vocab', split_axis=0, concat_...  92.3 us
    all_gather x1, blocking collectives, local(): panel_rows = lax.all_gather(head_weight, 'docs', axis=1, tiled=True)  49.2 us
    all_to_all x1, starting transfers between devices, local(): lax.all_to_all(send_sub, 'vocab', split_axis=0, concat_axis=0, tiled=True)  19.8 us
    all_to_all x1, waiting for transfers between devices, local(): lax.all_to_all(send_rows, 'vocab', split_axis=0, concat_axis=0, tiled=True)  13.4 us
    all_to_all x1, starting transfers between devices, local(): lax.all_to_all(lax.all_to_all(owner_terms, 'vocab', split_axis=0, concat_...  9.81 us
    all_to_all x1, waiting for transfers between devices, local(): lax.all_to_all(lax.all_to_all(send_rows, 'vocab', split_axis=0, concat_ax...  8.99 us
  transfers between devices with their start and end apart: 9, of which 6 were waited for; matrix products, arithmetic and copies ran while one was open for 18% of the time, Pallas kernels for 0%

profile of v1, /device:TPU:1, one launch (start us, length us, event | category | flops | bytes accessed | tf_op | source)
XLA Modules:
  0.0 441.7 jit_solution(930108816104330512)
XLA Ops:
  6.5 49.2 %all_gather.9 = bf16[128,1536]{0,1:T(8,128)(2,1)} all-gather(bf16[128,48]{0,1:T(8,128)(2,1)} %param.16), channel_id=1, replica_groups=mesh['vocab'=16,'docs'=32] {'docs'}, dimensions={1}, use_global_device_ids=true | all-gather | bytes 405504 | tf_op jit(solution)/shard_map/all_gather | solution.py:84
  55.8 0.8 copy.59
  56.5 0.1 eq.46
  56.6 0.1 eq.42
  56.8 0.1 copy.61
  56.9 0.3 fusion.5
  57.3 0.3 copy.62
  57.7 0.1 copy.58
  57.8 0.1 mul.48
  57.9 0.1 copy.63
  58.1 0.1 reshape.138
  58.2 0.3 fusion.4
  58.5 3.8 scatter_custom_fusion
  62.3 0.3 reshape.117
  62.5 0.8 copy.64
  63.3 19.8 %all-to-all-start = ((bf16[16,32,2]{1,2,0:T(2,128)(2,1)}), bf16[16,32,2]{1,2,0:T(2,128)(2,1)S(1)}, u32[]{:S(2)}, u32[]{:S(2)}) async-start(bf16[16,32,2]{1,2,0:T(2,128)(2,1)} %copy.64), calls=%async_computation | async-start | bytes 16384 | tf_op jit(solution)/shard_map/all_to_all | solution.py:55
  83.1 2.8 scatter_custom_fusion.1
  85.9 4.3 all-to-all-done
  90.2 4.0 all-to-all-start.2
  94.2 0.7 copy.65
  94.9 13.4 %all-to-all-done.2 = bf16[16,32,2,128]{3,2,1,0:T(2,128)(2,1)S(1)} async-done(((bf16[16,32,2,128]{3,2,1,0:T(2,128)(2,1)}), bf16[16,32,2,128]{3,2,1,0:T(2,128)(2,1)S(1)}, u32[]{:S(2)}, u32[]{:S(2)}) %all-to-all-start.2) | async-done | bytes 262176 | tf_op jit(solution)/shard_map/all_to_all | solution.py:48
  108.3 4.5 %all-to-all-start.1 = ((bf16[16,32,2]{0,2,1:T(2,128)(2,1)}), bf16[16,32,2]{0,2,1:T(2,128)(2,1)S(1)}, u32[]{:S(2)}, u32[]{:S(2)}) async-start(bf16[16,32,2]{0,2,1:T(2,128)(2,1)} %copy.65), calls=%async_computation.1 | async-start | bytes 32768 | tf_op jit(solution)/shard_map/all_to_all | solution.py:54
  112.8 0.9 copy.68
  113.7 7.8 %all-to-all-done.1 = bf16[16,32,2]{0,2,1:T(2,128)(2,1)S(1)} async-done(((bf16[16,32,2]{0,2,1:T(2,128)(2,1)}), bf16[16,32,2]{0,2,1:T(2,128)(2,1)S(1)}, u32[]{:S(2)}, u32[]{:S(2)}) %all-to-all-start.1) | async-done | bytes 2080 | tf_op jit(solution)/shard_map/all_to_all | solution.py:54
  121.5 3.9 all-to-all-start.3
  125.4 0.2 copy.67
  125.6 0.2 reshape.124
  125.8 0.2 fusion.12
  126.0 9.0 %all-to-all-done.3 = bf16[16,32,2,128]{3,2,0,1:T(2,128)(2,1)S(1)} async-done(((bf16[16,32,2,128]{3,2,0,1:T(2,128)(2,1)}), bf16[16,32,2,128]{3,2,0,1:T(2,128)(2,1)S(1)}, u32[]{:S(2)}, u32[]{:S(2)}) %all-to-all-start.3) | async-done | bytes 262176 | tf_op jit(solution)/shard_map/all_to_all | solution.py:47
  135.0 0.8 stack.2
  135.8 6.3 %all-to-all-start.6 = ((bf16[32,96,48]{1,2,0:T(8,128)(2,1)}), bf16[32,96,48]{1,2,0:T(8,128)(2,1)S(1)}, u32[]{:S(2)}, u32[]{:S(2)}) async-start(bf16[32,96,48]{1,2,0:T(8,128)(2,1)} %stack.2), calls=%async_computation.6 | async-start | bytes 786432 | tf_op jit(solution)/shard_map/all_to_all | solution.py:91
  142.1 0.2 copy.69
  142.3 3.5 broadcast_multiply_fusion
  145.8 8.3 %convolution_convert_fusion = bf16[1024,2048]{1,0:T(8,128)(2,1)} fusion(bf16[1024,2048]{1,0:T(8,128)(2,1)} %param.14, bf16[128,8,8,128]{3,2,1,0:T(8,128)(2,1)S(1)} %bitcast.29), kind=kOutput, calls=%fused_computation.3 | convolution fusion | flops 4297064448 | bytes 10485760 | tf_op jit(solution)/shard_map/dot_general | solution.py:68
  154.1 7.6 %reshape.120 = bf16[16,32,2,2048]{3,2,1,0:T(2,128)(2,1)} reshape(bf16[1024,2048]{1,0:T(8,128)(2,1)} %convolution_convert_fusion) | data formatting | bytes 8388608 | tf_op jit(solution)/shard_map/reshape | solution.py:71
  161.7 6.3 %all-to-all-start.4 = ((bf16[16,32,2,2048]{3,2,1,0:T(2,128)(2,1)}), bf16[16,32,2,2048]{3,2,1,0:T(2,128)(2,1)}, u32[]{:S(2)}, u32[]{:S(2)}) async-start(bf16[16,32,2,2048]{3,2,1,0:T(2,128)(2,1)} %reshape.120), calls=%async_computation.4 | async-start | bytes 8388608 | tf_op jit(solution)/shard_map/all_to_all | solution.py:73
  168.1 0.9 copy.72
  169.0 114.8 %all-to-all-done.4 = bf16[16,32,2,2048]{3,2,1,0:T(2,128)(2,1)} async-done(((bf16[16,32,2,2048]{3,2,1,0:T(2,128)(2,1)}), bf16[16,32,2,2048]{3,2,1,0:T(2,128)(2,1)}, u32[]{:S(2)}, u32[]{:S(2)}) %all-to-all-start.4) | async-done | bytes 4194336 | tf_op jit(solution)/shard_map/all_to_all | solution.py:73
  283.8 8.7 %copy.70 = bf16[16,32,2,2048]{3,2,0,1:T(2,128)(2,1)} copy(bf16[16,32,2,2048]{3,2,1,0:T(2,128)(2,1)} %all-to-all-done.4) | data formatting | bytes 8388608 | tf_op jit(solution)/shard_map/all_to_all | solution.py:73
  292.5 9.8 %all-to-all-start.5 = ((bf16[16,32,2,2048]{3,2,0,1:T(2,128)(2,1)}), bf16[16,32,2,2048]{3,2,0,1:T(2,128)(2,1)}, u32[]{:S(2)}, u32[]{:S(2)}) async-start(bf16[16,32,2,2048]{3,2,0,1:T(2,128)(2,1)} %copy.70), calls=%async_computation.5 | async-start | bytes 8388608 | tf_op jit(solution)/shard_map/all_to_all | solution.py:72
  302.4 92.3 %all-to-all-done.5 = bf16[16,32,2,2048]{3,2,0,1:T(2,128)(2,1)} async-done(((bf16[16,32,2,2048]{3,2,0,1:T(2,128)(2,1)}), bf16[16,32,2,2048]{3,2,0,1:T(2,128)(2,1)}, u32[]{:S(2)}, u32[]{:S(2)}) %all-to-all-start.5) | async-done | bytes 4194336 | tf_op jit(solution)/shard_map/all_to_all | solution.py:72
  394.7 8.0 %copy.71 = bf16[16,32,2,2048]{3,2,1,0:T(2,128)(2,1)} copy(bf16[16,32,2,2048]{3,2,0,1:T(2,128)(2,1)} %all-to-all-done.5) | data formatting | bytes 8388608 | tf_op jit(solution)/shard_map/all_to_all | solution.py:72
  402.8 7.2 %reshape.121 = bf16[1024,2048]{1,0:T(8,128)(2,1)} reshape(bf16[16,32,2,2048]{3,2,1,0:T(2,128)(2,1)} %copy.71) | data formatting | bytes 8388608 | tf_op jit(solution)/shard_map/reshape | solution.py:79
  409.9 7.1 %gather_fusion = bf16[512,2048]{1,0:T(8,128)(2,1)S(1)} fusion(bf16[1024,2048]{1,0:T(8,128)(2,1)} %reshape.121, s32[1024]{0:T(1024)S(1)} %pad_clamp_fusion), kind=kCustom, calls=%fused_computation | custom fusion | bytes 4196352 | tf_op jit(solution)/shard_map/gather | solution.py:80
  417.1 3.0 reshape.125
  420.1 4.8 %reduce_sum.19 = f32[128,2048]{1,0:T(8,128)S(1)} reduce(f32[128,4,2048]{2,1,0:T(4,128)} %reshape.125, f32[]{:T(128)} %constant.6.clone.1), dimensions={1}, to_apply=%region_5.6 | reduce | flops 786432 | bytes 5242884 | tf_op jit(solution)/shard_map/reduce_sum | solution.py:81
  425.0 5.1 %convolution_add_fusion.1 = f32[128,1536]{1,0:T(8,128)S(1)} fusion(bf16[2048,1536]{0,1:T(8,128)(2,1)} %all-gather.3.cloned.1.call-done, f32[128,2048]{1,0:T(8,128)S(1)} %reduce_sum.19, f32[2048]{0:T(1024)S(1)} %copy-done.4, f32[128]{0:T(128)S(1)} %convert_divide_fusion, f32[1536]{0:T(1024)S(1)} %copy-done.5), kind=kOutput, calls=%fused_computation.6 | convolution fusion | flops 807862272 | bytes 8141312 | tf_op jit(solution)/shard_map/dot_general | solution.py:85
  430.1 4.7 %fusion = bf16[128,1536]{1,0:T(8,128)(2,1)} fusion(f32[128,1536]{1,0:T(8,128)S(1)} %convolution_add_fusion.1, bf16[128,1536]{1,0:T(8,128)(2,1)S(1)} %copy-done, bf16[1536,1536]{1,0:T(8,128)(2,1)} %all-gather.5.cloned.1.call-done), kind=kOutput, calls=%fused_computation.7 | convolution fusion | flops 604372992 | bytes 6291456 | tf_op jit(solution)/shard_map/dot_general | solution.py:99
  (34 shorter events, 0.4 us)
Async XLA Ops:
  6.5 423.6 %copy-start = (bf16[128,1536]{1,0:T(8,128)(2,1)S(1)}, bf16[128,1536]{1,0:T(8,128)(2,1)}, u32[]{:S(2)}) copy-start(bf16[128,1536]{1,0:T(8,128)(2,1)} %param.19) | copy-start | bytes 1179652
  6.5 51.1 %copy-start.2 = (s32[128,4]{0,1:T(4,128)S(1)}, s32[128,4]{0,1:T(4,128)}, u32[]{:S(2)}) copy-start(s32[128,4]{0,1:T(4,128)} %param.11) | copy-start | bytes 6148
  6.5 51.4 %copy-start.3 = (s32[128,4]{0,1:T(4,128)S(1)}, s32[128,4]{0,1:T(4,128)}, u32[]{:S(2)}) copy-start(s32[128,4]{0,1:T(4,128)} %param.12) | copy-start | bytes 6148
  6.5 418.4 %all-gather.3.cloned.1.call-start = ((), (), s32[]{:S(2)}) async-start(), calls=%async_computation.7 | async-start | bytes 6684672 | tf_op jit(solution)/shard_map/all_gather | solution.py:87
  57.2 77.8 %copy-start.1 = (bf16[96,48]{0,1:T(8,128)(2,1)S(1)}, bf16[96,48]{0,1:T(8,128)(2,1)}, u32[]{:S(2)}) copy-start(bf16[96,48]{0,1:T(8,128)(2,1)} %param.18) | copy-start | bytes 27652
  63.3 26.9 %all-to-all-start = ((bf16[16,32,2]{1,2,0:T(2,128)(2,1)}), bf16[16,32,2]{1,2,0:T(2,128)(2,1)S(1)}, u32[]{:S(2)}, u32[]{:S(2)}) async-start(bf16[16,32,2]{1,2,0:T(2,128)(2,1)} %copy.64), calls=%async_computation | async-start | bytes 16384 | tf_op jit(solution)/shard_map/all_to_all | solution.py:55
  90.2 18.1 %all-to-all-start.2 = ((bf16[16,32,2,128]{3,2,1,0:T(2,128)(2,1)}), bf16[16,32,2,128]{3,2,1,0:T(2,128)(2,1)S(1)}, u32[]{:S(2)}, u32[]{:S(2)}) async-start(bf16[16,32,2,128]{3,2,1,0:T(2,128)(2,1)} %bitcast.6), calls=%async_computation.2 | async-start | bytes 524288 | tf_op jit(solution)/shard_map/all_to_all | solution.py:48
  108.3 13.2 %all-to-all-start.1 = ((bf16[16,32,2]{0,2,1:T(2,128)(2,1)}), bf16[16,32,2]{0,2,1:T(2,128)(2,1)S(1)}, u32[]{:S(2)}, u32[]{:S(2)}) async-start(bf16[16,32,2]{0,2,1:T(2,128)(2,1)} %copy.65), calls=%async_computation.1 | async-start | bytes 32768 | tf_op jit(solution)/shard_map/all_to_all | solution.py:54
  121.5 13.5 %all-to-all-start.3 = ((bf16[16,32,2,128]{3,2,0,1:T(2,128)(2,1)}), bf16[16,32,2,128]{3,2,0,1:T(2,128)(2,1)S(1)}, u32[]{:S(2)}, u32[]{:S(2)}) async-start(bf16[16,32,2,128]{3,2,0,1:T(2,128)(2,1)} %copy.68), calls=%async_computation.3 | async-start | bytes 524288 | tf_op jit(solution)/shard_map/all_to_all | solution.py:47
  135.8 25.9 %all-to-all-start.6 = ((bf16[32,96,48]{1,2,0:T(8,128)(2,1)}), bf16[32,96,48]{1,2,0:T(8,128)(2,1)S(1)}, u32[]{:S(2)}, u32[]{:S(2)}) async-start(bf16[32,96,48]{1,2,0:T(8,128)(2,1)} %stack.2), calls=%async_computation.6 | async-start | bytes 786432 | tf_op jit(solution)/shard_map/all_to_all | solution.py:91
  161.7 122.1 %all-to-all-start.4 = ((bf16[16,32,2,2048]{3,2,1,0:T(2,128)(2,1)}), bf16[16,32,2,2048]{3,2,1,0:T(2,128)(2,1)}, u32[]{:S(2)}, u32[]{:S(2)}) async-start(bf16[16,32,2,2048]{3,2,1,0:T(2,128)(2,1)} %reshape.120), calls=%async_computation.4 | async-start | bytes 8388608 | tf_op jit(solution)/shard_map/all_to_all | solution.py:73
  168.1 262.1 %all-gather.5.cloned.1.call-start = ((), (), s32[]{:S(2)}) async-start(), calls=%async_computation.8 | async-start | bytes 5013504 | tf_op jit(solution)/shard_map/all_gather | solution.py:101
  292.5 9.8 %copy-start.6 = (s32[128]{0:T(128)S(1)}, s32[128]{0:T(128)}, u32[]{:S(2)}) copy-start(s32[128]{0:T(128)} %param.13) | copy-start | bytes 1540
  292.5 102.2 %all-to-all-start.5 = ((bf16[16,32,2,2048]{3,2,0,1:T(2,128)(2,1)}), bf16[16,32,2,2048]{3,2,0,1:T(2,128)(2,1)}, u32[]{:S(2)}, u32[]{:S(2)}) async-start(bf16[16,32,2,2048]{3,2,0,1:T(2,128)(2,1)} %copy.70), calls=%async_computation.5 | async-start | bytes 8388608 | tf_op jit(solution)/shard_map/all_to_all | solution.py:72
  420.1 4.9 %copy-start.4 = (f32[2048]{0:T(1024)S(1)}, f32[2048]{0:T(1024)}, u32[]{:S(2)}) copy-start(f32[2048]{0:T(1024)} %param.15) | copy-start | bytes 24580
  420.1 4.9 %copy-start.5 = (f32[1536]{0:T(1024)S(1)}, f32[1536]{0:T(1024)}, u32[]{:S(2)}) copy-start(f32[1536]{0:T(1024)} %param.17) | copy-start | bytes 18436
Sparse Core Ops, SparseCore 0:
  55.9 74.2 all-gather.2
  171.0 111.6 all-gather.4
